TPU v7x, 32 devices: a whole 2x2x4 slice. The times are simulated.
32 devices in a mesh: section: 1, seq: 16 (over z, y, x), mp: 2 (over core).
Axes of the slice: x: 2, y: 2, z: 4, core: 2. Of those that a mesh axis runs over, the one named last changes fastest.
Arguments:
- hidden_in: bfloat16 [4096, 5376], P('seq'), may hold values from -30 to 30
- query_weight: bfloat16 [1, 5376, 2048], P('section', 'seq', 'mp'), may hold values from -0.078125 to 0.078125
- key_weight: bfloat16 [1, 5376, 1024], P('section', 'seq', 'mp'), may hold values from -0.078125 to 0.078125
- value_weight: bfloat16 [1, 5376, 1024], P('section', 'seq', 'mp'), may hold values from -0.078125 to 0.078125
- output_weight: bfloat16 [1, 2048, 5376], P('section', 'mp', 'seq'), may hold values from -0.5524272 to 0.5524272
- input_gain: bfloat16 [1, 5376], P('section'), may hold values from 0.099609375 to 1.8984375
- post_gain: bfloat16 [1, 5376], P('section', 'mp'), may hold values from 0.099609375 to 1.8984375
Outputs:
- hidden_out: bfloat16 [1, 4096, 5376], P('section', 'seq', 'mp')
All inputs are finite; a program needn't handle non-finite values.
Results may differ from a plain program's by a relative error of at most 0.013.
Values may be sent and summed in bfloat16 or wider, within the bound.
A program may use at most 128 MiB of HBM per device.

v0:
```python
import math

import jax
import jax.numpy as jnp
from jax import lax
from jax.sharding import PartitionSpec as P

HEADS = 16
KV_HEADS = 8
HEAD_DIM = 128
WINDOW = 1024
QSCALE = 168


NORM_EPS = 1e-06


def from_behind(block, axis, distance):
    devices = range(lax.axis_size(axis))
    route = [(i - distance, i) for i in devices if i - distance in devices]
    return lax.ppermute(block, axis, route)


def rope_tables(positions, head_size):
    half_dim = head_size // 2
    frequency = jnp.exp(
        -math.log(10000.0) * (2.0 * jnp.arange(half_dim, dtype=jnp.float32)) / head_size
    )
    angles = positions.astype(jnp.float32)[:, None] * frequency[None, :]
    return (jnp.cos(angles), jnp.sin(angles))


def norm_rotate(values, cosine, sine_table):
    scaled = values * lax.rsqrt(jnp.mean(values * values, axis=-1, keepdims=True) + NORM_EPS)
    half_dim = scaled.shape[-1] // 2
    leading = scaled[..., :half_dim]
    trailing = scaled[..., half_dim:]
    cosine = cosine[:, None, :]
    sine_table = sine_table[:, None, :]
    rotated = jnp.concatenate(
        [leading * cosine - trailing * sine_table, trailing * cosine + leading * sine_table],
        axis=-1,
    )
    return rotated.astype(jnp.bfloat16)


def body(hidden_in, query_weight, key_weight, value_weight, output_weight, input_gain, post_gain):
    row_count = hidden_in.shape[0]
    model_width = hidden_in.shape[1]
    half_width = post_gain.shape[1]
    core_index = lax.axis_index("mp")
    shard_index = lax.axis_index("seq")
    section_index = lax.axis_index("section")
    query_full, key_full, value_full = (
        lax.all_gather(query_weight[0], "seq", axis=0, tiled=True),
        lax.all_gather(key_weight[0], "seq", axis=0, tiled=True),
        lax.all_gather(value_weight[0], "seq", axis=0, tiled=True),
    )
    output_full = lax.all_gather(output_weight[0], "seq", axis=1, tiled=True)
    gain_first = input_gain[0].astype(jnp.float32)
    gain_second = post_gain[0].astype(jnp.float32)
    group_size = HEADS // KV_HEADS
    query_heads_local = query_full.shape[1] // HEAD_DIM
    local_heads = key_full.shape[1] // HEAD_DIM
    reach_shards = (WINDOW + row_count - 2) // row_count
    score_scale = 1.0 / math.sqrt(QSCALE)
    positions = shard_index * row_count + jnp.arange(row_count, dtype=jnp.int32)
    cosine, sine_table = rope_tables(positions, HEAD_DIM)
    key_positions = (
        shard_index * row_count
        - reach_shards * row_count
        + jnp.arange((reach_shards + 1) * row_count, dtype=jnp.int32)
    )
    distance = positions[:, None] - key_positions[None, :]
    visible = ((distance >= 0) & (distance < WINDOW) & (key_positions[None, :] >= 0)).astype(
        jnp.float32
    )

    def project_rows(full_rows):
        rows_float = full_rows.astype(jnp.float32)
        normed = (
            rows_float
            * lax.rsqrt(jnp.mean(rows_float * rows_float, axis=1, keepdims=True) + NORM_EPS)
            * gain_first
        ).astype(jnp.bfloat16)
        queries = jnp.dot(normed, query_full, preferred_element_type=jnp.float32)
        keys_raw = jnp.dot(normed, key_full, preferred_element_type=jnp.float32)
        values_raw = jnp.dot(normed, value_full, preferred_element_type=jnp.float32)
        query_heads = norm_rotate(
            queries.reshape(row_count, query_heads_local, HEAD_DIM), cosine, sine_table
        )
        key_heads = norm_rotate(
            keys_raw.reshape(row_count, local_heads, HEAD_DIM), cosine, sine_table
        )
        key_value = jnp.concatenate(
            [key_heads.reshape(row_count, -1), values_raw.astype(jnp.bfloat16)], axis=1
        )
        return (query_heads, key_value)

    def skip_rows(full_rows):
        return (
            jnp.zeros((row_count, query_heads_local, HEAD_DIM), jnp.bfloat16),
            jnp.zeros((row_count, 2 * local_heads * HEAD_DIM), jnp.bfloat16),
        )

    def attend_rows(query_heads, window_rows):
        window_count = window_rows.shape[0]
        key_block = window_rows[:, : local_heads * HEAD_DIM].reshape(
            window_count, local_heads, HEAD_DIM
        )
        value_block = window_rows[:, local_heads * HEAD_DIM :].reshape(
            window_count, local_heads, HEAD_DIM
        )
        grouped = query_heads.reshape(row_count, local_heads, group_size, HEAD_DIM)
        scores = (
            jnp.einsum("tkgd,skd->kgts", grouped, key_block, preferred_element_type=jnp.float32)
            * score_scale
        )
        weights_raw = jnp.exp(scores) * visible
        softmax_weights = (weights_raw / jnp.sum(weights_raw, axis=-1, keepdims=True)).astype(
            jnp.bfloat16
        )
        attended = jnp.einsum(
            "kgts,skd->tkgd", softmax_weights, value_block, preferred_element_type=jnp.float32
        )
        attended = attended.astype(jnp.bfloat16).reshape(row_count, -1)
        return jnp.dot(attended, output_full, preferred_element_type=jnp.float32)

    def skip_attend(query_heads, window_rows):
        return jnp.zeros((row_count, model_width), jnp.float32)

    def attend_layer(full_rows, residual_half, active):
        query_heads, key_value = lax.cond(active, project_rows, skip_rows, full_rows)
        pieces = [key_value]
        carried = key_value
        for offset in range(reach_shards):
            carried = from_behind(carried, "seq", 1)
            pieces = [carried] + pieces
        window_rows = jnp.concatenate(pieces, axis=0)
        partial_value = lax.cond(active, attend_rows, skip_attend, query_heads, window_rows)
        summed = lax.psum_scatter(
            partial_value.astype(jnp.bfloat16), "mp", scatter_dimension=1, tiled=True
        ).astype(jnp.float32)
        squares = lax.psum(jnp.sum(summed * summed, axis=1, keepdims=True), "mp")
        branch = summed * lax.rsqrt(squares / model_width + NORM_EPS) * gain_second
        return (residual_half.astype(jnp.float32) + branch).astype(jnp.bfloat16)

    own_half = lax.dynamic_slice_in_dim(hidden_in, core_index * half_width, half_width, 1)
    layer_one = attend_layer(hidden_in, own_half, section_index == 0)
    arrived = from_behind(layer_one, "section", 1)
    full_rows = lax.all_gather(arrived, "mp", axis=1, tiled=True)
    layer_two = attend_layer(full_rows, arrived, section_index == 1)
    result = jnp.where(section_index == 0, layer_one, layer_two)
    return result[None]


def solution(mesh):
    placed = (
        P("seq", None),
        P("section", "seq", "mp"),
        P("section", "seq", "mp"),
        P("section", "seq", "mp"),
        P("section", "mp", "seq"),
        P("section", None),
        P("section", "mp"),
    )
    return jax.shard_map(
        body, mesh=mesh, in_specs=placed, out_specs=P("section", "seq", "mp"), check_vma=False
    )
```

profile of v0, /device:TPU:9, one launch (start us, length us, event | category | flops | bytes accessed | tf_op | source)
XLA Modules:
  0.0 530.1 jit_solution(8867680530757714097)
XLA Ops:
  10.2 2.4 fusion.8
  13.2 83.8 %all-gather.9.cloned.1.call-done = bf16[1,5376,512]{2,1,0:T(8,128)(2,1)} async-done(((bf16[1,336,512]{2,1,0:T(8,128)(2,1)}), bf16[1,5376,512]{2,1,0:T(8,128)(2,1)}) %all-gather.9.cloned.1.call-update) | async-done | bytes 5505040 | tf_op jit(solution)/shard_map/all_gather | solution.py:56
  97.0 5.0 fusion.13
  104.8 80.6 %all-gather.11.cloned.1.call-done = bf16[1,5376,512]{2,1,0:T(8,128)(2,1)} async-done(((bf16[1,336,512]{2,1,0:T(8,128)(2,1)}), bf16[1,5376,512]{2,1,0:T(8,128)(2,1)}) %all-gather.11.cloned.1.call-update) | async-done | bytes 5505040 | tf_op jit(solution)/shard_map/all_gather | solution.py:57
  185.5 4.2 fusion.30
  189.7 3.1 collective-permute-start
  192.8 15.4 %collective-permute-done = bf16[256,1024]{1,0:T(8,128)(2,1)S(1)} collective-permute-done((bf16[256,1024]{1,0:T(8,128)(2,1)S(1)}, bf16[256,1024]{1,0:T(8,128)(2,1)S(1)}, u32[]{:S(2)}, u32[]{:S(2)}) %collective-permute-start) | collective-permute-done | bytes 524320 | tf_op jit(solution)/shard_map/ppermute | solution.py:21
  208.2 1.9 collective-permute-start.1
  210.1 20.4 %collective-permute-done.1 = bf16[256,1024]{1,0:T(8,128)(2,1)S(1)} collective-permute-done((bf16[256,1024]{1,0:T(8,128)(2,1)S(1)}, bf16[256,1024]{1,0:T(8,128)(2,1)S(1)}, u32[]{:S(2)}, u32[]{:S(2)}) %collective-permute-start.1) | collective-permute-done | bytes 524320 | tf_op jit(solution)/shard_map/ppermute | solution.py:21
  230.5 1.9 collective-permute-start.2
  232.5 25.3 %collective-permute-done.2 = bf16[256,1024]{1,0:T(8,128)(2,1)} collective-permute-done((bf16[256,1024]{1,0:T(8,128)(2,1)S(1)}, bf16[256,1024]{1,0:T(8,128)(2,1)}, u32[]{:S(2)}, u32[]{:S(2)}) %collective-permute-start.2) | collective-permute-done | bytes 524320 | tf_op jit(solution)/shard_map/ppermute | solution.py:21
  257.8 2.1 collective-permute-start.3
  260.3 19.2 %collective-permute-done.3 = bf16[256,1024]{1,0:T(8,128)(2,1)S(1)} collective-permute-done((bf16[256,1024]{1,0:T(8,128)(2,1)}, bf16[256,1024]{1,0:T(8,128)(2,1)S(1)}, u32[]{:S(2)}, u32[]{:S(2)}) %collective-permute-start.3) | collective-permute-done | bytes 524320 | tf_op jit(solution)/shard_map/ppermute | solution.py:21
  282.0 3.6 reshape.110
  287.0 65.3 %all-gather.13.cloned.1.call-done = bf16[1,5376,1024]{2,1,0:T(8,128)(2,1)} async-done(((bf16[1,336,1024]{2,1,0:T(8,128)(2,1)}), bf16[1,5376,1024]{2,1,0:T(8,128)(2,1)}) %all-gather.13.cloned.1.call-update) | async-done | bytes 11010064 | tf_op jit(solution)/shard_map/all_gather | solution.py:55
  352.2 6.7 %fusion.21 = f32[32,8,8,128]{3,1,2,0:T(8,128)S(1)} fusion(bf16[1,5376,1024]{2,1,0:T(8,128)(2,1)} %all-gather.13.cloned.1.call-done, bf16[256,5376]{1,0:T(8,128)(2,1)} %param.7, f32[5376]{0:T(1024)S(1)} %copy-done.4, f32[256]{0:T(256)S(1)} %add_rsqrt_fusion.3), kind=kOutput, calls=%fused_computation.27 | convolution fusion | flops 2824077312 | bytes 14833664 | tf_op jit(solution)/shard_map/cond/branch_1_fun/dot_general | solution.py:86
  361.4 2.6 fusion.4
  364.0 2.7 fusion.29
  366.7 123.0 %all-gather.15.cloned.1.call-done = bf16[1,1024,5376]{1,2,0:T(8,128)(2,1)} async-done(((bf16[1,1024,336]{1,2,0:T(8,128)(2,1)}), bf16[1,1024,5376]{1,2,0:T(8,128)(2,1)}) %all-gather.15.cloned.1.call-update) | async-done | bytes 11010064 | tf_op jit(solution)/shard_map/all_gather | solution.py:59
  489.7 11.6 %fusion.5 = bf16[256,5376]{1,0:T(8,128)(2,1)S(1)} fusion(bf16[256,1024]{0,1:T(8,128)(2,1)S(1)} %bitcast.66, bf16[1,1024,5376]{1,2,0:T(8,128)(2,1)} %all-gather.15.cloned.1.call-done), kind=kOutput, calls=%fused_computation.7 | convolution fusion | flops 2819948544 | bytes 14286848 | tf_op jit(solution)/shard_map/cond/branch_1_fun/dot_general | solution.py:127
  501.4 2.8 copy.45
  504.9 10.9 %reduce-scatter.4.cloned.1.call-done = bf16[2688,256]{1,0:T(8,128)(2,1)} async-done(((bf16[5376,256]{1,0:T(8,128)(2,1)}), bf16[2688,256]{1,0:T(8,128)(2,1)}) %reduce-scatter.4.cloned.1.call-update) | async-done | bytes 1376272
  518.0 2.5 psum.6
  520.5 3.1 fusion.20
  (58 shorter events, 16.6 us)
Async XLA Ops:
  6.5 90.4 %copy-start = (bf16[256,5376]{1,0:T(8,128)(2,1)S(1)}, bf16[256,5376]{1,0:T(8,128)(2,1)}, u32[]{:S(2)}) copy-start(bf16[256,5376]{1,0:T(8,128)(2,1)} %param.7) | copy-start | bytes 8257540
  6.5 90.4 %all-gather.9.cloned.1.call-start = ((), (), s32[]{:S(2)}) async-start(), calls=%async_computation.1 | async-start | bytes 5849088 | tf_op jit(solution)/shard_map/all_gather | solution.py:56
  7.3 178.2 %all-gather.11.cloned.1.call-start = ((), (), s32[]{:S(2)}) async-start(), calls=%async_computation.2 | async-start | bytes 5849088 | tf_op jit(solution)/shard_map/all_gather | solution.py:57
  8.0 344.2 %all-gather.13.cloned.1.call-start = ((), (), s32[]{:S(2)}) async-start(), calls=%async_computation.3 | async-start | bytes 11698176 | tf_op jit(solution)/shard_map/all_gather | solution.py:55
  8.7 481.0 %all-gather.15.cloned.1.call-start = ((), (), s32[]{:S(2)}) async-start(), calls=%async_computation.4 | async-start | bytes 11698176 | tf_op jit(solution)/shard_map/all_gather | solution.py:59
  9.3 506.6 %reduce-scatter.4.cloned.1.call-start = ((), (), s32[]{:S(2)}) async-start(), calls=%async_computation.5 | async-start | bytes 4128768
  10.2 86.8 %copy-start.3 = (f32[5376]{0:T(1024)}, f32[5376]{0:T(1024)S(1)}, u32[]{:S(2)}) copy-start(f32[5376]{0:T(1024)S(1)} %convert_reduce_fusion) | copy-start | bytes 64516
  189.7 18.5 %collective-permute-start = (bf16[256,1024]{1,0:T(8,128)(2,1)S(1)}, bf16[256,1024]{1,0:T(8,128)(2,1)S(1)}, u32[]{:S(2)}, u32[]{:S(2)}) collective-permute-start(bf16[256,1024]{1,0:T(8,128)(2,1)S(1)} %pad_maximum_fusion), channel_id=1, source_target_pairs={{0,2},{2,4},{4,6},{6,8},{8,10},{10,12},{12,14},{14,16},{16,18},{18... | collective-permute-start | bytes 1572872 | tf_op jit(solution)/shard_map/ppermute | solution.py:21
  208.2 22.3 %collective-permute-start.1 = (bf16[256,1024]{1,0:T(8,128)(2,1)S(1)}, bf16[256,1024]{1,0:T(8,128)(2,1)S(1)}, u32[]{:S(2)}, u32[]{:S(2)}) collective-permute-start(bf16[256,1024]{1,0:T(8,128)(2,1)S(1)} %collective-permute-done), channel_id=1, source_target_pairs={{0,2},{2,4},{4,6},{6,8},{8,10},{10,12},{12,14},{14,16},{16,18},{18... | collective-permute-start | bytes 1572872 | tf_op jit(solution)/shard_map/ppermute | solution.py:21
  230.5 27.2 %collective-permute-start.2 = (bf16[256,1024]{1,0:T(8,128)(2,1)S(1)}, bf16[256,1024]{1,0:T(8,128)(2,1)}, u32[]{:S(2)}, u32[]{:S(2)}) collective-permute-start(bf16[256,1024]{1,0:T(8,128)(2,1)S(1)} %collective-permute-done.1), channel_id=1, source_target_pairs={{0,2},{2,4},{4,6},{6,8},{8,10},{10,12},{12,14},{14,16},{16,18},{18... | collective-permute-start | bytes 1572872 | tf_op jit(solution)/shard_map/ppermute | solution.py:21
  257.8 21.7 %collective-permute-start.3 = (bf16[256,1024]{1,0:T(8,128)(2,1)}, bf16[256,1024]{1,0:T(8,128)(2,1)S(1)}, u32[]{:S(2)}, u32[]{:S(2)}) collective-permute-start(bf16[256,1024]{1,0:T(8,128)(2,1)} %collective-permute-done.2), channel_id=1, source_target_pairs={{0,2},{2,4},{4,6},{6,8},{8,10},{10,12},{12,14},{14,16},{16,18},{18... | collective-permute-start | bytes 1572872 | tf_op jit(solution)/shard_map/ppermute | solution.py:21
  282.0 70.3 %copy-start.4 = (f32[5376]{0:T(1024)S(1)}, f32[5376]{0:T(1024)}, u32[]{:S(2)}) copy-start(f32[5376]{0:T(1024)} %copy-done.3) | copy-start | bytes 64516
  360.1 1.3 copy-start.1
  361.4 2.6 copy-start.2
  504.2 0.7 copy-start.5
Sparse Core Ops, SparseCore 0:
  10.2 86.7 all-gather.8
  99.7 85.6 all-gather.10
  188.3 163.9 all-gather.12
  354.9 134.7 all-gather.14
  504.3 11.4 reduce-scatter.3
where the time goes:
time: 532 us; the launch traced here: 530 us
  waiting for transfers between devices  447 us (84%)
  matrix products  32.8 us (6%)
  local copies, waits for them, and re-layouts  15.2 us (3%)
  between operations  13.4 us (3%)
  other arithmetic  10.5 us (2%)
  starting transfers between devices  9.15 us (2%)
    all_gather x1, waiting for transfers between devices, body(): output_full = lax.all_gather(output_weight[0], 'seq', axis=1, tiled=True)  123 us
    all_gather x1, waiting for transfers between devices, body(): lax.all_gather(key_weight[0], 'seq', axis=0, tiled=True)  83.8 us
    all_gather x1, waiting for transfers between devices, body(): lax.all_gather(value_weight[0], 'seq', axis=0, tiled=True)  80.6 us
    ppermute x4, waiting for transfers between devices, from_behind(): return lax.ppermute(block, axis, route)  80.3 us
    all_gather x1, waiting for transfers between devices, body(): lax.all_gather(query_weight[0], 'seq', axis=0, tiled=True)  65.3 us
    unnamed x6, waiting for transfers between devices  13.6 us
    dot_general x1, matrix products, attend_rows(): return jnp.dot(attended, output_full, preferred_element_type=jnp.float32)  11.6 us
  transfers between devices with their start and end apart: 9, of which 9 were waited for; matrix products, arithmetic and copies ran while one was open for 7% of the time, Pallas kernels for 0%

commit v1 on v0

v1 whole, which is shorter than its diff:
```python
import functools
import math

import jax
import jax.numpy as jnp
from jax import lax
from jax.experimental import pallas as pl
from jax.experimental.pallas import tpu as pltpu
from jax.sharding import PartitionSpec as P

HEADS = 16
KV_HEADS = 8
HEAD_DIM = 128
WINDOW = 1024
QSCALE = 168


NORM_EPS = 1e-06
MESH = pl.DeviceIdType.MESH


def from_behind(block, axis, distance):
    devices = range(lax.axis_size(axis))
    route = [(i - distance, i) for i in devices if i - distance in devices]
    return lax.ppermute(block, axis, route)


def rope_tables(positions, head_size):
    half_dim = head_size // 2
    frequency = jnp.exp(
        -math.log(10000.0) * (2.0 * jnp.arange(half_dim, dtype=jnp.float32)) / head_size
    )
    angles = positions.astype(jnp.float32)[:, None] * frequency[None, :]
    return (jnp.cos(angles), jnp.sin(angles))


def place(group_size):
    shard = lax.axis_index("seq")
    return lax.div(shard, group_size), lax.rem(shard, group_size), lax.axis_index("mp")


def gather_kernel(
    groups, group_size, rows_ref, query_ref, key_ref, value_ref,
    weights_ref, tokens_ref,
    own_sem, plane_send, plane_recv, token_send, token_recv, twin_send, twin_recv,
    up_send, up_recv, down_send, down_recv,
):
    group, member, core = place(group_size)
    here = group * group_size
    shard = here + member
    barrier = pltpu.get_barrier_semaphore()
    for d in range(1, group_size):
        peer = here + lax.rem(member + d, group_size)
        pl.semaphore_signal(barrier, inc=1, device_id={"seq": peer}, device_id_type=MESH)
    pl.semaphore_signal(barrier, inc=1, device_id={"mp": 1 - core}, device_id_type=MESH)
    above = shard + group_size
    below = shard - group_size

    @pl.when(group > 0)
    def _():
        pl.semaphore_signal(barrier, inc=1, device_id={"seq": below}, device_id_type=MESH)

    @pl.when(group < groups - 1)
    def _():
        pl.semaphore_signal(barrier, inc=1, device_id={"seq": above}, device_id_type=MESH)

    pl.semaphore_wait(
        barrier,
        group_size + jnp.where(group > 0, 1, 0) + jnp.where(group < groups - 1, 1, 0),
    )

    sources = (query_ref, key_ref, value_ref)
    widths = [ref.shape[1] // group_size for ref in sources]
    starts = [0, widths[0], widths[0] + widths[1]]

    def piece(part, index):
        width = widths[part]
        return sources[part].at[:, pl.ds(pl.multiple_of(index * width, width), width)]

    def slot(block, part):
        return weights_ref.at[block, :, pl.ds(starts[part], widths[part])]

    own = [
        pltpu.make_async_copy(piece(part, member), slot(shard, part), own_sem.at[part])
        for part in range(3)
    ]
    for copy in own:
        copy.start()
    plane = []
    for d in range(1, group_size):
        index = lax.rem(member + d, group_size)
        for part in range(3):
            copy = pltpu.make_async_remote_copy(
                src_ref=piece(part, index),
                dst_ref=slot(shard, part),
                send_sem=plane_send.at[d - 1, part],
                recv_sem=plane_recv.at[d - 1, part],
                device_id={"seq": here + index},
                device_id_type=MESH,
            )
            copy.start()
            plane.append(copy)
    own_rows = pltpu.make_async_copy(rows_ref, tokens_ref.at[member], own_sem.at[3])
    own_rows.start()
    token_copies = []
    for d in range(1, group_size):
        index = lax.rem(member + d, group_size)
        copy = pltpu.make_async_remote_copy(
            src_ref=rows_ref.at[core],
            dst_ref=tokens_ref.at[member, core],
            send_sem=token_send.at[d - 1],
            recv_sem=token_recv.at[d - 1],
            device_id={"seq": here + index},
            device_id_type=MESH,
        )
        copy.start()
        token_copies.append(copy)

    def relay(step, d, upward):
        origin = group - step + 1 if upward else group + step - 1
        block = origin * group_size + lax.rem(member - d + group_size, group_size)
        send, recv = (up_send, up_recv) if upward else (down_send, down_recv)
        return pltpu.make_async_remote_copy(
            src_ref=weights_ref.at[block],
            dst_ref=weights_ref.at[block],
            send_sem=send.at[step - 1, d],
            recv_sem=recv.at[step - 1, d],
            device_id={"seq": above if upward else below},
            device_id_type=MESH,
        )

    def arrival(step, d, upward):
        origin = group - step if upward else group + step
        block = origin * group_size + lax.rem(member - d + group_size, group_size)
        send, recv = (up_send, up_recv) if upward else (down_send, down_recv)
        return pltpu.make_async_remote_copy(
            src_ref=weights_ref.at[block],
            dst_ref=weights_ref.at[block],
            send_sem=send.at[step - 1, d],
            recv_sem=recv.at[step - 1, d],
            device_id={"seq": above if upward else below},
            device_id_type=MESH,
        )

    def sends(step, upward):
        if upward:
            return (group < groups - 1) & (group - step + 1 >= 0)
        return (group > 0) & (group + step - 1 <= groups - 1)

    def receives(step, upward):
        return group - step >= 0 if upward else group + step <= groups - 1

    twins = []
    for step in range(1, groups):
        for d in range(group_size):
            if step == 1:
                if d == 0:
                    for copy in own:
                        copy.wait()
                else:
                    for part in range(3):
                        origin = here + lax.rem(member - d + group_size, group_size)
                        pltpu.make_async_remote_copy(
                            src_ref=piece(part, member),
                            dst_ref=slot(origin, part),
                            send_sem=plane_send.at[d - 1, part],
                            recv_sem=plane_recv.at[d - 1, part],
                            device_id={"seq": origin},
                            device_id_type=MESH,
                        ).wait_recv()
            for upward in (True, False):
                if step > 1:

                    @pl.when(receives(step - 1, upward))
                    def _():
                        arrival(step - 1, d, upward).wait_recv()

                @pl.when(sends(step, upward))
                def _():
                    relay(step, d, upward).start()

        if step == 1:
            for d in range(1, group_size):
                origin = lax.rem(member - d + group_size, group_size)
                pltpu.make_async_remote_copy(
                    src_ref=rows_ref.at[core],
                    dst_ref=tokens_ref.at[origin, core],
                    send_sem=token_send.at[d - 1],
                    recv_sem=token_recv.at[d - 1],
                    device_id={"seq": here + origin},
                    device_id_type=MESH,
                ).wait_recv()
                copy = pltpu.make_async_remote_copy(
                    src_ref=tokens_ref.at[origin, core],
                    dst_ref=tokens_ref.at[origin, core],
                    send_sem=twin_send.at[d - 1],
                    recv_sem=twin_recv.at[d - 1],
                    device_id={"mp": 1 - core},
                    device_id_type=MESH,
                )
                copy.start()
                twins.append(copy)

    own_rows.wait()
    for copy in plane + token_copies:
        copy.wait_send()
    for d in range(1, group_size):
        origin = lax.rem(member - d + group_size, group_size)
        twins[d - 1].wait_send()
        pltpu.make_async_remote_copy(
            src_ref=tokens_ref.at[origin, 1 - core],
            dst_ref=tokens_ref.at[origin, 1 - core],
            send_sem=twin_send.at[d - 1],
            recv_sem=twin_recv.at[d - 1],
            device_id={"mp": 1 - core},
            device_id_type=MESH,
        ).wait_recv()
    for step in range(1, groups):
        for d in range(group_size):
            for upward in (True, False):

                @pl.when(sends(step, upward))
                def _():
                    relay(step, d, upward).wait_send()

                if step == groups - 1:

                    @pl.when(receives(step, upward))
                    def _():
                        arrival(step, d, upward).wait_recv()


def gather(rows, query_weight, key_weight, value_weight, group_size):
    shards = lax.axis_size("seq")
    groups = shards // group_size
    depth = query_weight.shape[0]
    width = (query_weight.shape[1] + key_weight.shape[1] + value_weight.shape[1]) // group_size
    row_count, model_width = rows.shape
    halves = rows.reshape(2, row_count // 2, model_width)
    dma = pltpu.SemaphoreType.DMA
    anywhere = pl.BlockSpec(memory_space=pl.ANY)
    weights, tokens = pl.pallas_call(
        functools.partial(gather_kernel, groups, group_size),
        out_shape=(
            jax.ShapeDtypeStruct((shards, depth, width), jnp.bfloat16),
            jax.ShapeDtypeStruct((group_size,) + halves.shape, jnp.bfloat16),
        ),
        in_specs=[anywhere] * 4,
        out_specs=(anywhere, anywhere),
        scratch_shapes=[
            dma((4,)),
            dma((group_size - 1, 3)),
            dma((group_size - 1, 3)),
            dma((group_size - 1,)),
            dma((group_size - 1,)),
            dma((group_size - 1,)),
            dma((group_size - 1,)),
            dma((groups - 1, group_size)),
            dma((groups - 1, group_size)),
            dma((groups - 1, group_size)),
            dma((groups - 1, group_size)),
        ],
        compiler_params=pltpu.CompilerParams(collective_id=0, has_side_effects=True),
        name="gather",
    )(halves, query_weight, key_weight, value_weight)
    return weights.reshape(shards * depth, width), tokens.reshape(-1, model_width)


def attend_kernel(
    groups, group_size, row_count, projected_ref, cosine_ref, sine_ref, out_ref,
    query_ref, window_ref, sent_ref, halo_send, halo_recv, send_sem, recv_sem,
):
    group, member, core = place(group_size)
    here = group * group_size
    shard = here + member
    above = shard + group_size
    below = shard - group_size
    barrier = pltpu.get_barrier_semaphore()
    for d in range(1, group_size):
        peer = here + lax.rem(member + d, group_size)
        pl.semaphore_signal(barrier, inc=1, device_id={"seq": peer}, device_id_type=MESH)

    @pl.when(group > 0)
    def _():
        pl.semaphore_signal(barrier, inc=1, device_id={"seq": below}, device_id_type=MESH)

    @pl.when(group < groups - 1)
    def _():
        pl.semaphore_signal(barrier, inc=1, device_id={"seq": above}, device_id_type=MESH)

    pl.semaphore_wait(
        barrier,
        group_size - 1 + jnp.where(group > 0, 1, 0) + jnp.where(group < groups - 1, 1, 0),
    )
    span = group_size * row_count
    query_width = query_ref.shape[1]
    query_heads = query_width // HEAD_DIM

    def rotated(block):
        scaled = block * lax.rsqrt(jnp.mean(block * block, axis=-1, keepdims=True) + NORM_EPS)
        turned = pltpu.roll(scaled, HEAD_DIM // 2, 1)
        return (scaled * cosine_ref[...] + turned * sine_ref[...]).astype(jnp.bfloat16)

    window_ref[pl.ds(span, span), :HEAD_DIM] = rotated(
        projected_ref[:, query_width : query_width + HEAD_DIM]
    )
    window_ref[pl.ds(span, span), HEAD_DIM:] = projected_ref[
        :, query_width + HEAD_DIM :
    ].astype(jnp.bfloat16)
    halo = pltpu.make_async_remote_copy(
        src_ref=window_ref.at[pl.ds(span, span)],
        dst_ref=window_ref.at[pl.ds(0, span)],
        send_sem=halo_send,
        recv_sem=halo_recv,
        device_id={"seq": above},
        device_id_type=MESH,
    )

    @pl.when(group < groups - 1)
    def _():
        halo.start()

    for head in range(query_heads):
        columns = slice(head * HEAD_DIM, (head + 1) * HEAD_DIM)
        query_ref[:, columns] = rotated(projected_ref[:, columns])

    @pl.when(group == 0)
    def _():
        window_ref[pl.ds(0, span), :] = jnp.zeros((span, window_ref.shape[1]), jnp.bfloat16)

    @pl.when(group > 0)
    def _():
        halo.wait_recv()

    reach = span + row_count
    query_pos = lax.broadcasted_iota(jnp.int32, (row_count, reach), 0) + span
    key_pos = lax.broadcasted_iota(jnp.int32, (row_count, reach), 1)
    distance = query_pos - key_pos
    near = (distance >= 0) & (distance < WINDOW)
    score_scale = 1.0 / math.sqrt(QSCALE)
    copies = []
    for turn in range(1, group_size + 1):
        index = lax.rem(member + turn, group_size)
        first = pl.multiple_of(index * row_count, row_count)
        keys = window_ref[pl.ds(first, reach), :HEAD_DIM]
        values = window_ref[pl.ds(first, reach), HEAD_DIM:]
        visible = near & (key_pos + first + group * span >= span)
        for head in range(query_heads):
            columns = slice(head * HEAD_DIM, (head + 1) * HEAD_DIM)
            scores = lax.dot_general(
                query_ref[pl.ds(first, row_count), columns], keys,
                (((1,), (1,)), ((), ())), preferred_element_type=jnp.float32,
            )
            raw = jnp.where(visible, jnp.exp(scores * score_scale), 0.0)
            probs = (raw * (1.0 / jnp.sum(raw, axis=-1, keepdims=True))).astype(jnp.bfloat16)
            sent_ref[turn - 1, :, columns] = jnp.dot(
                probs, values, preferred_element_type=jnp.float32
            ).astype(jnp.bfloat16)
        mine = out_ref.at[:, pl.ds(pl.multiple_of(member * query_width, query_width), query_width)]
        if turn < group_size:
            copy = pltpu.make_async_remote_copy(
                src_ref=sent_ref.at[turn - 1],
                dst_ref=mine,
                send_sem=send_sem.at[turn - 1],
                recv_sem=recv_sem.at[turn - 1],
                device_id={"seq": here + index},
                device_id_type=MESH,
            )
        else:
            copy = pltpu.make_async_copy(sent_ref.at[turn - 1], mine, send_sem.at[turn - 1])
        copy.start()
        copies.append(copy)
    copies[-1].wait()
    for turn in range(1, group_size):
        copies[turn - 1].wait_send()
        origin = lax.rem(member - turn + group_size, group_size)
        pltpu.make_async_remote_copy(
            src_ref=sent_ref.at[turn - 1],
            dst_ref=out_ref.at[
                :, pl.ds(pl.multiple_of(origin * query_width, query_width), query_width)
            ],
            send_sem=send_sem.at[turn - 1],
            recv_sem=recv_sem.at[turn - 1],
            device_id={"seq": here + origin},
            device_id_type=MESH,
        ).wait_recv()

    @pl.when(group < groups - 1)
    def _():
        halo.wait_send()


def attend(projected, cosine, sine, group_size):
    groups = lax.axis_size("seq") // group_size
    span = projected.shape[0]
    row_count = span // group_size
    query_width = projected.shape[1] - 2 * HEAD_DIM
    dma = pltpu.SemaphoreType.DMA
    vmem = pl.BlockSpec(memory_space=pltpu.VMEM)
    return pl.pallas_call(
        functools.partial(attend_kernel, groups, group_size, row_count),
        out_shape=jax.ShapeDtypeStruct((row_count, group_size * query_width), jnp.bfloat16),
        in_specs=[vmem] * 3,
        out_specs=vmem,
        scratch_shapes=[
            pltpu.VMEM((span, query_width), jnp.bfloat16),
            pltpu.VMEM((2 * span, 2 * HEAD_DIM), jnp.bfloat16),
            pltpu.VMEM((group_size, row_count, query_width), jnp.bfloat16),
            dma,
            dma,
            dma((group_size,)),
            dma((group_size - 1,)),
        ],
        compiler_params=pltpu.CompilerParams(
            collective_id=1, has_side_effects=True, vmem_limit_bytes=40 * 1024 * 1024
        ),
        name="attend",
    )(projected, cosine, sine)


def body(hidden_in, query_weight, key_weight, value_weight, output_weight, input_gain, post_gain):
    row_count, model_width = hidden_in.shape
    half_width = post_gain.shape[1]
    core_index = lax.axis_index("mp")
    shard_index = lax.axis_index("seq")
    section_index = lax.axis_index("section")
    sections = lax.axis_size("section")
    shards = lax.axis_size("seq")
    group_size = key_weight.shape[2] // HEAD_DIM
    gain_first = input_gain[0].astype(jnp.float32)
    gain_second = post_gain[0].astype(jnp.float32)
    output_full = lax.all_gather(output_weight[0], "seq", axis=1, tiled=True)
    span = group_size * row_count
    positions = (shard_index // group_size) * span + jnp.arange(span, dtype=jnp.int32)
    cosine, sine = rope_tables(positions, HEAD_DIM)
    cosine = jnp.concatenate([cosine, cosine], axis=1)
    sine = jnp.concatenate([-sine, sine], axis=1)

    def normed_rows(full_rows):
        rows_float = full_rows.astype(jnp.float32)
        return (
            rows_float
            * lax.rsqrt(jnp.mean(rows_float * rows_float, axis=1, keepdims=True) + NORM_EPS)
            * gain_first
        ).astype(jnp.bfloat16)

    def attend_layer(weights, tokens, residual_half):
        projected = jnp.dot(tokens, weights, preferred_element_type=jnp.float32)
        attended = attend(projected, cosine, sine, group_size)
        partial_value = jnp.dot(attended, output_full, preferred_element_type=jnp.float32)
        summed = lax.psum_scatter(
            partial_value.astype(jnp.bfloat16), "mp", scatter_dimension=1, tiled=True
        ).astype(jnp.float32)
        squares = lax.psum(jnp.sum(summed * summed, axis=1, keepdims=True), "mp")
        branch = summed * lax.rsqrt(squares / model_width + NORM_EPS) * gain_second
        return (residual_half.astype(jnp.float32) + branch).astype(jnp.bfloat16)

    own_half = lax.dynamic_slice_in_dim(hidden_in, core_index * half_width, half_width, 1)
    weights, tokens = gather(
        normed_rows(hidden_in), query_weight[0], key_weight[0], value_weight[0], group_size
    )
    layer = attend_layer(weights, tokens, own_half)
    result = layer
    plane = [
        list(range(first, first + group_size)) for first in range(0, shards, group_size)
    ]
    for step in range(1, sections):
        arrived = from_behind(layer, "section", 1)
        rows = normed_rows(lax.all_gather(arrived, "mp", axis=1, tiled=True))
        tokens = lax.all_gather(rows, "seq", axis=0, tiled=True, axis_index_groups=plane)
        layer = attend_layer(weights, tokens, arrived)
        result = jnp.where(section_index == step, layer, result)
    return result[None]


def solution(mesh):
    placed = (
        P("seq", None),
        P("section", "seq", "mp"),
        P("section", "seq", "mp"),
        P("section", "seq", "mp"),
        P("section", "mp", "seq"),
        P("section", None),
        P("section", "mp"),
    )
    return jax.shard_map(
        body, mesh=mesh, in_specs=placed, out_specs=P("section", "seq", "mp"), check_vma=False
    )
```

time: 532 us -> 315 us (0.59)
  waiting for transfers between devices: 447 us -> 12.6 us
  Pallas kernels: 0 us -> 242 us
  matrix products: 32.8 us -> 22.9 us
  starting transfers between devices: 9.15 us -> 0.04 us
  local copies, waits for them, and re-layouts: 15.2 us -> 7.8 us
    pallas_call x0 -> x2, Pallas kernels: none -> 242 us  [the longest x1 219 us: gather(): pl.pallas_call(functools.partial(gather_kernel, groups, group_size), out_...]
    all_gather x3 -> x0, waiting for transfers between devices: 230 us -> none  [the longest x1 83.8 us: body(): lax.all_gather(key_weight[0], 'seq', axis=0, tiled=True)]
    all_gather x1, waiting for transfers between devices: 123 us -> 0.02 us  [body(): output_full = lax.all_gather(output_weight[0], 'seq', axis=1, tiled=True)]
    ppermute x4 -> x0, waiting for transfers between devices: 80.3 us -> none  [from_behind(): return lax.ppermute(block, axis, route)]
    dot_general x6 -> x2, matrix products: 32.8 us -> 22.9 us  [the longest x1 12.7 us: attend_layer(): jnp.dot(attended, output_full, preferred_element_type=jnp.float32)]
    ppermute x4 -> x0, starting transfers between devices: 8.99 us -> none  [from_behind(): return lax.ppermute(block, axis, route)]
    reshape x3 -> x0, local copies, waits for them, and re-layouts: 6.22 us -> none  [the longest x1 3.58 us: attend_rows(): window_rows[:, :local_heads * HEAD_DIM]]
    unnamed x6 -> x3, waiting for transfers between devices: 13.6 us -> 12.6 us
  transfers between devices with their start and end apart: 9 -> 2, of which waited for: 9 -> 1; matrix products, arithmetic and copies ran while one was open for 7% -> 6% of each run, Pallas kernels for 0% -> 77%
where the time goes in v1:
time: 315 us; the launch traced here: 314 us
  Pallas kernels  242 us (77%)
  matrix products  22.9 us (7%)
  between operations  13.5 us (4%)
  other arithmetic  12.7 us (4%)
  waiting for transfers between devices  12.6 us (4%)
  local copies, waits for them, and re-layouts  7.8 us (2%)
    pallas_call x1, Pallas kernels, gather(): pl.pallas_call(functools.partial(gather_kernel, groups, group_size), out_...  219 us
    pallas_call x1, Pallas kernels, attend(): pl.pallas_call(functools.partial(attend_kernel, groups, group_size, row_c...  22.6 us
    dot_general x1, matrix products, attend_layer(): jnp.dot(attended, output_full, preferred_element_type=jnp.float32)  12.7 us
    unnamed x3, waiting for transfers between devices  12.6 us
    dot_general x1, matrix products, attend_layer(): projected = jnp.dot(tokens, weights, preferred_element_type=jnp.float32)  10.2 us
    unnamed x6, local copies, waits for them, and re-layouts  7.8 us
  transfers between devices with their start and end apart: 2, of which 1 were waited for; matrix products, arithmetic and copies ran while one was open for 6% of the time, Pallas kernels for 77%

profile of v1, /device:TPU:9, one launch (start us, length us, event | category | flops | bytes accessed | tf_op | source)
XLA Modules:
  0.0 313.8 jit_solution(1732030759552178812)
XLA Ops:
  6.5 0.0 copy-start
  6.5 0.0 all-gather.3.cloned.1.call-start
  6.5 0.7 all-gather.3.cloned.1.call-update
  7.3 0.0 reduce-scatter.4.cloned.1.call-start
  7.3 0.8 convert_reduce_fusion
  8.2 2.4 fusion.5
  10.6 0.0 copy-done
  10.6 2.4 fusion.7
  12.9 219.1 %gather.1 = (bf16[16,336,512]{2,1,0:T(8,128)(2,1)}, bf16[4,2,128,5376]{3,2,1,0:T(8,128)(2,1)}) custom-call(bf16[2,128,5376]{2,1,0:T(8,128)(2,1)} %bitcast.21, bf16[336,1024]{1,0:T(8,128)(2,1)} %bitcast.23, bf16[336,512]{1,0:T(8,128)(2,1)} %bitcast.24, bf16[336,512]{1,0:T(8,128)(2,1)} %bitcast.25), custom_call_target="tpu_custom_call" | custom-call | tf_op jit(solution)/shard_map/gather/pallas_call | solution.py:242
  232.1 1.9 fusion.13
  234.0 0.3 pad_maximum_fusion
  234.4 10.2 %fusion.14.projected_ref = f32[1024,512]{1,0:T(8,128)S(1)} fusion(bf16[1024,5376]{1,0:T(8,128)(2,1)} %bitcast.28, bf16[5376,512]{1,0:T(8,128)(2,1)} %bitcast.29), kind=kOutput, calls=%fused_computation.26 | convolution fusion | flops 5637144576 | bytes 18612224 | tf_op jit(solution)/shard_map/dot_general | solution.py:448
  244.6 22.6 %attend.1 = bf16[256,1024]{1,0:T(8,128)(2,1)S(1)} custom-call(f32[1024,512]{1,0:T(8,128)S(1)} %fusion.14.projected_ref, f32[1024,128]{1,0:T(8,128)S(1)} %get-tuple-element.12.cosine_ref, f32[1024,128]{1,0:T(8,128)S(1)} %get-tuple-element.13.sine_ref), custom_call_target="tpu_custom_call" | custom-call | tf_op jit(solution)/shard_map/attend/pallas_call | solution.py:400
  267.2 0.0 all-gather.3.cloned.1.call-done
  267.3 12.7 %fusion.2 = bf16[256,5376]{1,0:T(8,128)(2,1)} fusion(bf16[256,1024]{1,0:T(8,128)(2,1)S(1)} %attend.1, bf16[1,1024,5376]{1,2,0:T(8,128)(2,1)} %all-gather.3.cloned.1.call-done), kind=kOutput, calls=%fused_computation.2 | convolution fusion | flops 2819948544 | bytes 14286848 | tf_op jit(solution)/shard_map/dot_general | solution.py:450
  279.9 4.6 %copy.8 = bf16[256,5376]{0,1:T(8,128)(2,1)} copy(bf16[256,5376]{1,0:T(8,128)(2,1)} %fusion.2) | data formatting | bytes 5505024
  284.6 0.0 copy-start.1
  284.6 0.0 reduce-scatter.4.cloned.1.call-update
  284.6 0.7 copy-done.1
  285.3 11.8 %reduce-scatter.4.cloned.1.call-done = bf16[2688,256]{1,0:T(8,128)(2,1)} async-done(((bf16[5376,256]{1,0:T(8,128)(2,1)}), bf16[2688,256]{1,0:T(8,128)(2,1)}) %reduce-scatter.4.cloned.1.call-update) | async-done | bytes 1376272
  297.1 2.5 copy.9
  299.6 1.7 fusion.8
  301.3 2.5 psum.7
  303.8 3.1 fusion.12
  (5 shorter events, 0.1 us)
Async XLA Ops:
  6.5 4.0 %copy-start = (bf16[256,5376]{1,0:T(8,128)(2,1)S(1)}, bf16[256,5376]{1,0:T(8,128)(2,1)}, u32[]{:S(2)}) copy-start(bf16[256,5376]{1,0:T(8,128)(2,1)} %param.7) | copy-start | bytes 8257540
  6.5 260.7 %all-gather.3.cloned.1.call-start = ((), (), s32[]{:S(2)}) async-start(), calls=%async_computation.1 | async-start | bytes 11698176 | tf_op jit(solution)/shard_map/all_gather | solution.py:432
  7.3 289.9 %reduce-scatter.4.cloned.1.call-start = ((), (), s32[]{:S(2)}) async-start(), calls=%async_computation.2 | async-start | bytes 4128768
  284.6 0.7 copy-start.1
Sparse Core Ops, SparseCore 0:
  10.2 198.9 all-gather.2
  284.7 12.3 reduce-scatter.3

commit v2 on v1

--- a/solution.py
+++ b/solution.py
@@ -40,10 +40,11 @@
 
 
 def gather_kernel(
-    groups, group_size, rows_ref, query_ref, key_ref, value_ref,
-    weights_ref, tokens_ref,
+    groups, group_size, rows_ref, query_ref, key_ref, value_ref, mix_ref,
+    weights_ref, tokens_ref, mixes_ref,
     own_sem, plane_send, plane_recv, token_send, token_recv, twin_send, twin_recv,
     up_send, up_recv, down_send, down_recv,
+    side_send, side_recv, pass_send, pass_recv,
 ):
     group, member, core = place(group_size)
     here = group * group_size
@@ -102,19 +103,130 @@
             plane.append(copy)
     own_rows = pltpu.make_async_copy(rows_ref, tokens_ref.at[member], own_sem.at[3])
     own_rows.start()
-    token_copies = []
-    for d in range(1, group_size):
-        index = lax.rem(member + d, group_size)
-        copy = pltpu.make_async_remote_copy(
+    own_mix = pltpu.make_async_copy(mix_ref, mixes_ref.at[shard], own_sem.at[4])
+    own_mix.start()
+
+    def flipped(bits):
+        low = lax.rem(member, 2)
+        high = member - low
+        if bits & 1:
+            low = 1 - low
+        if bits & 2:
+            high = 2 - high
+        return high + low
+
+    half_columns = rows_ref.shape[2] // 2
+
+    def token_direct(bits, sender):
+        return pltpu.make_async_remote_copy(
             src_ref=rows_ref.at[core],
-            dst_ref=tokens_ref.at[member, core],
-            send_sem=token_send.at[d - 1],
-            recv_sem=token_recv.at[d - 1],
-            device_id={"seq": here + index},
-            device_id_type=MESH,
-        )
-        copy.start()
-        token_copies.append(copy)
+            dst_ref=tokens_ref.at[sender, core],
+            send_sem=token_send.at[bits - 1],
+            recv_sem=token_recv.at[bits - 1],
+            device_id={"seq": here + flipped(bits)},
+            device_id_type=MESH,
+        )
+
+    def token_half(owner, which, bits):
+        part = tokens_ref.at[owner, core, :, pl.ds(which * half_columns, half_columns)]
+        return pltpu.make_async_remote_copy(
+            src_ref=part,
+            dst_ref=part,
+            send_sem=token_send.at[2 + which],
+            recv_sem=token_recv.at[2 + which],
+            device_id={"seq": here + flipped(bits)},
+            device_id_type=MESH,
+        )
+
+    def twin(index, half):
+        if index < 2:
+            part = tokens_ref.at[flipped(index + 1), half]
+        else:
+            part = tokens_ref.at[
+                flipped(3), half, :, pl.ds((index - 2) * half_columns, half_columns)
+            ]
+        return pltpu.make_async_remote_copy(
+            src_ref=part,
+            dst_ref=part,
+            send_sem=twin_send.at[index],
+            recv_sem=twin_recv.at[index],
+            device_id={"mp": 1 - core},
+            device_id_type=MESH,
+        )
+
+    token_direct(1, member).start()
+    token_direct(2, member).start()
+
+    mix_half = mix_ref.shape[1] // 2
+
+    def mix_side(origin, bits, owner, own):
+        block = mixes_ref.at[origin * group_size + owner]
+        return pltpu.make_async_remote_copy(
+            src_ref=mix_ref if own else block,
+            dst_ref=block,
+            send_sem=side_send.at[bits - 1, origin],
+            recv_sem=side_recv.at[bits - 1, origin],
+            device_id={"seq": here + flipped(bits)},
+            device_id_type=MESH,
+        )
+
+    def mix_pass(origin, owner, which, bits):
+        part = mixes_ref.at[
+            origin * group_size + owner, :, pl.ds(which * mix_half, mix_half)
+        ]
+        return pltpu.make_async_remote_copy(
+            src_ref=part,
+            dst_ref=part,
+            send_sem=pass_send.at[which, origin],
+            recv_sem=pass_recv.at[which, origin],
+            device_id={"seq": here + flipped(bits)},
+            device_id_type=MESH,
+        )
+
+    def mix_line(step, upward, origin):
+        send, recv = (up_send, up_recv) if upward else (down_send, down_recv)
+        block = mixes_ref.at[origin * group_size + member]
+        return pltpu.make_async_remote_copy(
+            src_ref=mix_ref if step == 1 else block,
+            dst_ref=block,
+            send_sem=send.at[step - 1, group_size],
+            recv_sem=recv.at[step - 1, group_size],
+            device_id={"seq": above if upward else below},
+            device_id_type=MESH,
+        )
+
+    def pass_on(origin):
+        mix_side(origin, 1, flipped(1), False).wait_recv()
+        mix_pass(origin, flipped(1), 0, 2).start()
+        mix_side(origin, 2, flipped(2), False).wait_recv()
+        mix_pass(origin, flipped(2), 1, 1).start()
+
+    def mix_step(step):
+        for upward in (True, False):
+
+            @pl.when(receives(step, upward))
+            def _():
+                origin = group - step if upward else group + step
+                if step > 0:
+                    mix_line(step, upward, origin).wait_recv()
+                if step < groups - 1:
+
+                    @pl.when(sends(step + 1, upward))
+                    def _():
+                        mix_line(step + 1, upward, origin).start()
+
+                if step > 0 or upward:
+                    mix_side(origin, 1, member, step == 0).start()
+                    mix_side(origin, 2, member, step == 0).start()
+
+        if step == 1:
+            pass_on(group)
+        elif step > 1:
+            for upward in (True, False):
+
+                @pl.when(receives(step - 1, upward))
+                def _():
+                    pass_on(group - step + 1 if upward else group + step - 1)
 
     def relay(step, d, upward):
         origin = group - step + 1 if upward else group + step - 1
@@ -150,7 +262,7 @@
     def receives(step, upward):
         return group - step >= 0 if upward else group + step <= groups - 1
 
-    twins = []
+    mix_step(0)
     for step in range(1, groups):
         for d in range(group_size):
             if step == 1:
@@ -180,41 +292,50 @@
                     relay(step, d, upward).start()
 
         if step == 1:
-            for d in range(1, group_size):
-                origin = lax.rem(member - d + group_size, group_size)
-                pltpu.make_async_remote_copy(
-                    src_ref=rows_ref.at[core],
-                    dst_ref=tokens_ref.at[origin, core],
-                    send_sem=token_send.at[d - 1],
-                    recv_sem=token_recv.at[d - 1],
-                    device_id={"seq": here + origin},
-                    device_id_type=MESH,
-                ).wait_recv()
-                copy = pltpu.make_async_remote_copy(
-                    src_ref=tokens_ref.at[origin, core],
-                    dst_ref=tokens_ref.at[origin, core],
-                    send_sem=twin_send.at[d - 1],
-                    recv_sem=twin_recv.at[d - 1],
-                    device_id={"mp": 1 - core},
-                    device_id_type=MESH,
-                )
-                copy.start()
-                twins.append(copy)
+            token_direct(1, flipped(1)).wait_recv()
+            token_half(flipped(1), 0, 2).start()
+            twin(0, core).start()
+            token_direct(2, flipped(2)).wait_recv()
+            token_half(flipped(2), 1, 1).start()
+            twin(1, core).start()
+        mix_step(step)
+        if step == 1:
+            token_half(flipped(3), 0, 2).wait_recv()
+            twin(2, core).start()
+            token_half(flipped(3), 1, 1).wait_recv()
+            twin(3, core).start()
+
+    for upward in (True, False):
+
+        @pl.when(receives(groups - 1, upward))
+        def _():
+            pass_on(group - groups + 1 if upward else group + groups - 1)
 
     own_rows.wait()
-    for copy in plane + token_copies:
+    own_mix.wait()
+    for copy in plane:
         copy.wait_send()
-    for d in range(1, group_size):
-        origin = lax.rem(member - d + group_size, group_size)
-        twins[d - 1].wait_send()
-        pltpu.make_async_remote_copy(
-            src_ref=tokens_ref.at[origin, 1 - core],
-            dst_ref=tokens_ref.at[origin, 1 - core],
-            send_sem=twin_send.at[d - 1],
-            recv_sem=twin_recv.at[d - 1],
-            device_id={"mp": 1 - core},
-            device_id_type=MESH,
-        ).wait_recv()
+    for bits in (1, 2):
+        token_direct(bits, member).wait_send()
+    token_half(flipped(1), 0, 2).wait_send()
+    token_half(flipped(2), 1, 1).wait_send()
+    for index in range(4):
+        twin(index, core).wait_send()
+        twin(index, 1 - core).wait_recv()
+    for origin in range(groups):
+        mix_side(origin, 1, member, False).wait_send()
+        mix_side(origin, 2, member, False).wait_send()
+        mix_pass(origin, flipped(1), 0, 2).wait_send()
+        mix_pass(origin, flipped(2), 1, 1).wait_send()
+        mix_pass(origin, flipped(3), 0, 2).wait_recv()
+        mix_pass(origin, flipped(3), 1, 1).wait_recv()
+    for step in range(1, groups):
+        for upward in (True, False):
+
+            @pl.when(sends(step, upward))
+            def _():
+                mix_line(step, upward, group).wait_send()
+
     for step in range(1, groups):
         for d in range(group_size):
             for upward in (True, False):
@@ -230,7 +351,7 @@
                         arrival(step, d, upward).wait_recv()
 
 
-def gather(rows, query_weight, key_weight, value_weight, group_size):
+def gather(rows, query_weight, key_weight, value_weight, mix_weight, group_size):
     shards = lax.axis_size("seq")
     groups = shards // group_size
     depth = query_weight.shape[0]
@@ -239,31 +360,40 @@
     halves = rows.reshape(2, row_count // 2, model_width)
     dma = pltpu.SemaphoreType.DMA
     anywhere = pl.BlockSpec(memory_space=pl.ANY)
-    weights, tokens = pl.pallas_call(
+    weights, tokens, mixes = pl.pallas_call(
         functools.partial(gather_kernel, groups, group_size),
         out_shape=(
             jax.ShapeDtypeStruct((shards, depth, width), jnp.bfloat16),
             jax.ShapeDtypeStruct((group_size,) + halves.shape, jnp.bfloat16),
+            jax.ShapeDtypeStruct((shards,) + mix_weight.shape, jnp.bfloat16),
         ),
-        in_specs=[anywhere] * 4,
-        out_specs=(anywhere, anywhere),
+        in_specs=[anywhere] * 5,
+        out_specs=(anywhere, anywhere, anywhere),
         scratch_shapes=[
-            dma((4,)),
+            dma((5,)),
             dma((group_size - 1, 3)),
             dma((group_size - 1, 3)),
-            dma((group_size - 1,)),
-            dma((group_size - 1,)),
-            dma((group_size - 1,)),
-            dma((group_size - 1,)),
-            dma((groups - 1, group_size)),
-            dma((groups - 1, group_size)),
-            dma((groups - 1, group_size)),
-            dma((groups - 1, group_size)),
+            dma((4,)),
+            dma((4,)),
+            dma((4,)),
+            dma((4,)),
+            dma((groups - 1, group_size + 1)),
+            dma((groups - 1, group_size + 1)),
+            dma((groups - 1, group_size + 1)),
+            dma((groups - 1, group_size + 1)),
+            dma((2, groups)),
+            dma((2, groups)),
+            dma((2, groups)),
+            dma((2, groups)),
         ],
         compiler_params=pltpu.CompilerParams(collective_id=0, has_side_effects=True),
         name="gather",
-    )(halves, query_weight, key_weight, value_weight)
-    return weights.reshape(shards * depth, width), tokens.reshape(-1, model_width)
+    )(halves, query_weight, key_weight, value_weight, mix_weight)
+    return (
+        weights.reshape(shards * depth, width),
+        tokens.reshape(-1, model_width),
+        mixes.reshape(-1, mix_weight.shape[1]),
+    )
 
 
 def attend_kernel(
@@ -418,6 +548,73 @@
     )(projected, cosine, sine)
 
 
+def finish_kernel(
+    partial_ref, residual_ref, gain_ref, out_ref, other_ref, total_ref, mine_ref, theirs_ref,
+    send_sem, recv_sem,
+):
+    core = lax.axis_index("mp")
+    barrier = pltpu.get_barrier_semaphore()
+    pl.semaphore_signal(barrier, inc=1, device_id={"mp": 1 - core}, device_id_type=MESH)
+    pl.semaphore_wait(barrier, 1)
+    half = residual_ref.shape[1]
+
+    def columns(index):
+        return pl.ds(pl.multiple_of(index * half, 128), half)
+
+    copy = pltpu.make_async_remote_copy(
+        src_ref=partial_ref.at[:, columns(1 - core)],
+        dst_ref=other_ref,
+        send_sem=send_sem.at[0],
+        recv_sem=recv_sem.at[0],
+        device_id={"mp": 1 - core},
+        device_id_type=MESH,
+    )
+    copy.start()
+    copy.wait()
+    total_ref[...] = partial_ref[:, columns(core)].astype(jnp.float32) + other_ref[...].astype(
+        jnp.float32
+    )
+    squares = jnp.sum(total_ref[...] * total_ref[...], axis=1, keepdims=True)
+    mine_ref[...] = jnp.broadcast_to(squares, mine_ref.shape)
+    copy = pltpu.make_async_remote_copy(
+        src_ref=mine_ref,
+        dst_ref=theirs_ref,
+        send_sem=send_sem.at[1],
+        recv_sem=recv_sem.at[1],
+        device_id={"mp": 1 - core},
+        device_id_type=MESH,
+    )
+    copy.start()
+    copy.wait()
+    mean = (mine_ref[:, :1] + theirs_ref[:, :1]) / (2 * half)
+    branch = total_ref[...] * lax.rsqrt(mean + NORM_EPS) * gain_ref[...]
+    out_ref[...] = (residual_ref[...].astype(jnp.float32) + branch).astype(jnp.bfloat16)
+
+
+def finish(partial_value, residual, gain):
+    row_count, half = residual.shape
+    dma = pltpu.SemaphoreType.DMA
+    vmem = pl.BlockSpec(memory_space=pltpu.VMEM)
+    return pl.pallas_call(
+        finish_kernel,
+        out_shape=jax.ShapeDtypeStruct((row_count, half), jnp.bfloat16),
+        in_specs=[vmem] * 3,
+        out_specs=vmem,
+        scratch_shapes=[
+            pltpu.VMEM((row_count, half), jnp.bfloat16),
+            pltpu.VMEM((row_count, half), jnp.float32),
+            pltpu.VMEM((row_count, 128), jnp.float32),
+            pltpu.VMEM((row_count, 128), jnp.float32),
+            dma((2,)),
+            dma((2,)),
+        ],
+        compiler_params=pltpu.CompilerParams(
+            collective_id=2, has_side_effects=True, vmem_limit_bytes=40 * 1024 * 1024
+        ),
+        name="finish",
+    )(partial_value, residual, gain.reshape(1, half))
+
+
 def body(hidden_in, query_weight, key_weight, value_weight, output_weight, input_gain, post_gain):
     row_count, model_width = hidden_in.shape
     half_width = post_gain.shape[1]
@@ -429,7 +626,6 @@
     group_size = key_weight.shape[2] // HEAD_DIM
     gain_first = input_gain[0].astype(jnp.float32)
     gain_second = post_gain[0].astype(jnp.float32)
-    output_full = lax.all_gather(output_weight[0], "seq", axis=1, tiled=True)
     span = group_size * row_count
     positions = (shard_index // group_size) * span + jnp.arange(span, dtype=jnp.int32)
     cosine, sine = rope_tables(positions, HEAD_DIM)
@@ -447,17 +643,19 @@
     def attend_layer(weights, tokens, residual_half):
         projected = jnp.dot(tokens, weights, preferred_element_type=jnp.float32)
         attended = attend(projected, cosine, sine, group_size)
-        partial_value = jnp.dot(attended, output_full, preferred_element_type=jnp.float32)
-        summed = lax.psum_scatter(
-            partial_value.astype(jnp.bfloat16), "mp", scatter_dimension=1, tiled=True
-        ).astype(jnp.float32)
-        squares = lax.psum(jnp.sum(summed * summed, axis=1, keepdims=True), "mp")
-        branch = summed * lax.rsqrt(squares / model_width + NORM_EPS) * gain_second
-        return (residual_half.astype(jnp.float32) + branch).astype(jnp.bfloat16)
+        partial_value = lax.dot_general(
+            attended, mixes, (((1,), (1,)), ((), ())), preferred_element_type=jnp.float32
+        ).astype(jnp.bfloat16)
+        return finish(partial_value, residual_half, gain_second)
 
     own_half = lax.dynamic_slice_in_dim(hidden_in, core_index * half_width, half_width, 1)
-    weights, tokens = gather(
-        normed_rows(hidden_in), query_weight[0], key_weight[0], value_weight[0], group_size
+    weights, tokens, mixes = gather(
+        normed_rows(hidden_in),
+        query_weight[0],
+        key_weight[0],
+        value_weight[0],
+        output_weight[0].T,
+        group_size,
     )
     layer = attend_layer(weights, tokens, own_half)
     result = layer

time: 315 us -> 216 us (0.69)
  Pallas kernels: 242 us -> 182 us
  between operations: 13.5 us -> 0.12 us
  waiting for transfers between devices: 12.6 us -> 0 us
  local copies, waits for them, and re-layouts: 7.8 us -> 2.53 us
    pallas_call x1, Pallas kernels: 219 us -> 152 us  [gather(): pl.pallas_call(functools.partial(gather_kernel, groups, group_size), out_...]
    unnamed x3 -> x0, waiting for transfers between devices: 12.6 us -> none
    pallas_call x0 -> x1, Pallas kernels: none -> 8.38 us  [finish(): pl.pallas_call(finish_kernel, out_shape=jax.ShapeDtypeStruct((row_count,...]
    unnamed x6 -> x3, local copies, waits for them, and re-layouts: 7.8 us -> 1.09 us
  transfers between devices with their start and end apart: 2 -> 0, of which waited for: 1 -> 0; matrix products, arithmetic and copies ran while one was open for 6% -> 0% of each run, Pallas kernels for 77% -> 0%
where the time goes in v2:
time: 216 us
  Pallas kernels  182 us (84%)
  matrix products  21.8 us (10%)
  other arithmetic  9.6 us (4%)
  local copies, waits for them, and re-layouts  2.53 us (1%)
    pallas_call x1, Pallas kernels, gather(): pl.pallas_call(functools.partial(gather_kernel, groups, group_size), out_...  152 us
    pallas_call x1, Pallas kernels, attend(): pl.pallas_call(functools.partial(attend_kernel, groups, group_size, row_c...  21.4 us
    dot_general x1, matrix products, attend_layer(): lax.dot_general(attended, mixes, (((1,), (1,)), ((), ())), preferred_elem...  11.5 us
    dot_general x1, matrix products, attend_layer(): projected = jnp.dot(tokens, weights, preferred_element_type=jnp.float32)  10.2 us
    pallas_call x1, Pallas kernels, finish(): pl.pallas_call(finish_kernel, out_shape=jax.ShapeDtypeStruct((row_count,...  8.38 us

profile of v2, /device:TPU:9, one launch (start us, length us, event | category | flops | bytes accessed | tf_op | source)
XLA Modules:
  0.0 215.6 jit_solution(14535831481556024106)
XLA Ops:
  0.0 0.8 convert_reduce_fusion
  0.8 2.4 %fusion = f32[256]{0:T(256)S(1)} fusion(bf16[256,5376]{1,0:T(8,128)(2,1)} %param.7), kind=kLoop, calls=%fused_computation.3 | loop fusion | flops 4128512 | bytes 2753536 | tf_op jit(solution)/shard_map/reduce_sum | solution.py:639
  3.2 4.1 %fusion.2 = bf16[256,5376]{1,0:T(8,128)(2,1)} fusion(bf16[256,5376]{1,0:T(8,128)(2,1)} %param.7, f32[5376]{0:T(1024)S(1)} %convert_reduce_fusion, f32[256]{0:T(256)S(1)} %add_rsqrt_fusion), kind=kLoop, calls=%fused_computation.5 | loop fusion | flops 5505024 | bytes 5527552 | tf_op jit(solution)/shard_map/convert_element_type | solution.py:641
  7.3 151.7 %gather.1 = (bf16[16,336,512]{2,1,0:T(8,128)(2,1)}, bf16[4,2,128,5376]{3,2,1,0:T(8,128)(2,1)}, bf16[16,336,1024]{2,1,0:T(8,128)(2,1)}) custom-call(bf16[2,128,5376]{2,1,0:T(8,128)(2,1)} %bitcast.16, bf16[336,1024]{1,0:T(8,128)(2,1)} %bitcast.17, bf16[336,512]{1,0:T(8,128)(2,1)} %bitcast.19, bf16[336,512]{1,0:T(8,128)(2,1)} %bitcast.20, ...), custom_call_target="tpu_custom_call" | custom-call | tf_op jit(solution)/shard_map/gather/pallas_call | solution.py:363
  159.1 10.2 %fusion.4.projected_ref = f32[1024,512]{1,0:T(8,128)S(1)} fusion(bf16[1024,5376]{1,0:T(8,128)(2,1)} %bitcast.22, bf16[5376,512]{1,0:T(8,128)(2,1)} %bitcast.23), kind=kOutput, calls=%fused_computation.16 | convolution fusion | flops 5637144576 | bytes 18612224 | tf_op jit(solution)/shard_map/dot_general | solution.py:644
  169.4 1.9 fusion.3
  171.3 0.3 pad_maximum_fusion
  171.6 21.4 %attend.1 = bf16[256,1024]{1,0:T(8,128)(2,1)S(1)} custom-call(f32[1024,512]{1,0:T(8,128)S(1)} %fusion.4.projected_ref, f32[1024,128]{1,0:T(8,128)S(1)} %get-tuple-element.14.cosine_ref, f32[1024,128]{1,0:T(8,128)S(1)} %get-tuple-element.15.sine_ref), custom_call_target="tpu_custom_call" | custom-call | tf_op jit(solution)/shard_map/attend/pallas_call | solution.py:530
  193.1 0.0 copy-start
  193.1 11.5 %convolution_convert_fusion.partial_ref = bf16[256,5376]{1,0:T(8,128)(2,1)S(1)} fusion(bf16[256,1024]{1,0:T(8,128)(2,1)S(1)} %attend.1, bf16[5376,1024]{1,0:T(8,128)(2,1)} %bitcast.21), kind=kOutput, calls=%fused_computation | convolution fusion | flops 2819948544 | bytes 14286848 | tf_op jit(solution)/shard_map/dot_general | solution.py:646
  204.6 1.4 constant_dynamic-slice_fusion.residual_ref
  206.1 0.0 copy-done
  206.1 8.4 %finish.1 = bf16[256,2688]{1,0:T(8,128)(2,1)S(1)} custom-call(bf16[256,5376]{1,0:T(8,128)(2,1)S(1)} %convolution_convert_fusion.partial_ref, bf16[256,2688]{1,0:T(8,128)(2,1)S(1)} %constant_dynamic-slice_fusion.residual_ref, f32[1,2688]{1,0:T(1,128)S(1)} %convert_element_type.26.gain_ref), custom_call_target="tpu_custom_call" | custom-call | tf_op jit(solution)/shard_map/finish/pallas_call | solution.py:598
  214.5 1.1 copy.9
  (4 shorter events, 0.0 us)
Async XLA Ops:
  193.1 13.0 %copy-start = (bf16[1,2688]{1,0:T(2,128)(2,1)S(1)}, bf16[1,2688]{1,0:T(2,128)(2,1)}, u32[]{:S(2)}) copy-start(bf16[1,2688]{1,0:T(2,128)(2,1)} %param.13) | copy-start | bytes 16132

commit v3 on v2

--- a/solution.py
+++ b/solution.py
@@ -40,11 +40,11 @@
 
 
 def gather_kernel(
-    groups, group_size, rows_ref, query_ref, key_ref, value_ref, mix_ref,
+    groups, group_size, hidden_ref, gain_ref, query_ref, key_ref, value_ref, mix_ref,
     weights_ref, tokens_ref, mixes_ref,
     own_sem, plane_send, plane_recv, token_send, token_recv, twin_send, twin_recv,
     up_send, up_recv, down_send, down_recv,
-    side_send, side_recv, pass_send, pass_recv,
+    side_send, side_recv, pass_send, pass_recv, rows_ref,
 ):
     group, member, core = place(group_size)
     here = group * group_size
@@ -101,8 +101,6 @@
             )
             copy.start()
             plane.append(copy)
-    own_rows = pltpu.make_async_copy(rows_ref, tokens_ref.at[member], own_sem.at[3])
-    own_rows.start()
     own_mix = pltpu.make_async_copy(mix_ref, mixes_ref.at[shard], own_sem.at[4])
     own_mix.start()
 
@@ -154,8 +152,6 @@
             device_id_type=MESH,
         )
 
-    token_direct(1, member).start()
-    token_direct(2, member).start()
 
     mix_half = mix_ref.shape[1] // 2
 
@@ -263,6 +259,20 @@
         return group - step >= 0 if upward else group + step <= groups - 1
 
     mix_step(0)
+    chunk = 16
+    for half in range(2):
+
+        @pl.loop(0, rows_ref.shape[1] // chunk)
+        def _(index):
+            at = pl.ds(pl.multiple_of(index * chunk, chunk), chunk)
+            values = hidden_ref[half, at, :].astype(jnp.float32)
+            scale = lax.rsqrt(jnp.mean(values * values, axis=1, keepdims=True) + NORM_EPS)
+            rows_ref[half, at, :] = (values * scale * gain_ref[...]).astype(jnp.bfloat16)
+
+    token_direct(1, member).start()
+    token_direct(2, member).start()
+    own_rows = pltpu.make_async_copy(rows_ref, tokens_ref.at[member], own_sem.at[3])
+    own_rows.start()
     for step in range(1, groups):
         for d in range(group_size):
             if step == 1:
@@ -351,7 +361,7 @@
                         arrival(step, d, upward).wait_recv()
 
 
-def gather(rows, query_weight, key_weight, value_weight, mix_weight, group_size):
+def gather(rows, gain, query_weight, key_weight, value_weight, mix_weight, group_size):
     shards = lax.axis_size("seq")
     groups = shards // group_size
     depth = query_weight.shape[0]
@@ -367,7 +377,7 @@
             jax.ShapeDtypeStruct((group_size,) + halves.shape, jnp.bfloat16),
             jax.ShapeDtypeStruct((shards,) + mix_weight.shape, jnp.bfloat16),
         ),
-        in_specs=[anywhere] * 5,
+        in_specs=[pl.BlockSpec(memory_space=pltpu.VMEM)] * 2 + [anywhere] * 4,
         out_specs=(anywhere, anywhere, anywhere),
         scratch_shapes=[
             dma((5,)),
@@ -385,10 +395,13 @@
             dma((2, groups)),
             dma((2, groups)),
             dma((2, groups)),
+            pltpu.VMEM(halves.shape, jnp.bfloat16),
         ],
-        compiler_params=pltpu.CompilerParams(collective_id=0, has_side_effects=True),
+        compiler_params=pltpu.CompilerParams(
+            collective_id=0, has_side_effects=True, vmem_limit_bytes=32 * 1024 * 1024
+        ),
         name="gather",
-    )(halves, query_weight, key_weight, value_weight, mix_weight)
+    )(halves, gain.reshape(1, model_width), query_weight, key_weight, value_weight, mix_weight)
     return (
         weights.reshape(shards * depth, width),
         tokens.reshape(-1, model_width),
@@ -397,8 +410,9 @@
 
 
 def attend_kernel(
-    groups, group_size, row_count, projected_ref, cosine_ref, sine_ref, out_ref,
-    query_ref, window_ref, sent_ref, halo_send, halo_recv, send_sem, recv_sem,
+    groups, group_size, row_count, projected_ref, cosine_ref, sine_ref, mixes_ref, partial_ref,
+    query_ref, window_ref, sent_ref, out_ref, held_ref,
+    halo_send, halo_recv, send_sem, recv_sem, held_sem,
 ):
     group, member, core = place(group_size)
     here = group * group_size
@@ -422,6 +436,8 @@
         barrier,
         group_size - 1 + jnp.where(group > 0, 1, 0) + jnp.where(group < groups - 1, 1, 0),
     )
+    held = pltpu.make_async_copy(mixes_ref, held_ref, held_sem)
+    held.start()
     span = group_size * row_count
     query_width = query_ref.shape[1]
     query_heads = query_width // HEAD_DIM
@@ -437,18 +453,21 @@
     window_ref[pl.ds(span, span), HEAD_DIM:] = projected_ref[
         :, query_width + HEAD_DIM :
     ].astype(jnp.bfloat16)
-    halo = pltpu.make_async_remote_copy(
-        src_ref=window_ref.at[pl.ds(span, span)],
-        dst_ref=window_ref.at[pl.ds(0, span)],
-        send_sem=halo_send,
-        recv_sem=halo_recv,
-        device_id={"seq": above},
-        device_id_type=MESH,
-    )
+
+    def halo(index):
+        return pltpu.make_async_remote_copy(
+            src_ref=window_ref.at[pl.ds(span + index * row_count, row_count)],
+            dst_ref=window_ref.at[pl.ds(index * row_count, row_count)],
+            send_sem=halo_send.at[index],
+            recv_sem=halo_recv.at[index],
+            device_id={"seq": above},
+            device_id_type=MESH,
+        )
 
     @pl.when(group < groups - 1)
     def _():
-        halo.start()
+        for index in reversed(range(group_size)):
+            halo(index).start()
 
     for head in range(query_heads):
         columns = slice(head * HEAD_DIM, (head + 1) * HEAD_DIM)
@@ -457,10 +476,6 @@
     @pl.when(group == 0)
     def _():
         window_ref[pl.ds(0, span), :] = jnp.zeros((span, window_ref.shape[1]), jnp.bfloat16)
-
-    @pl.when(group > 0)
-    def _():
-        halo.wait_recv()
 
     reach = span + row_count
     query_pos = lax.broadcasted_iota(jnp.int32, (row_count, reach), 0) + span
@@ -468,10 +483,31 @@
     distance = query_pos - key_pos
     near = (distance >= 0) & (distance < WINDOW)
     score_scale = 1.0 / math.sqrt(QSCALE)
-    copies = []
-    for turn in range(1, group_size + 1):
-        index = lax.rem(member + turn, group_size)
-        first = pl.multiple_of(index * row_count, row_count)
+
+    def exchange(index, origin):
+        return pltpu.make_async_remote_copy(
+            src_ref=sent_ref.at[index],
+            dst_ref=out_ref.at[
+                :, pl.ds(pl.multiple_of(origin * query_width, query_width), query_width)
+            ],
+            send_sem=send_sem.at[index],
+            recv_sem=recv_sem.at[origin],
+            device_id={"seq": here + index},
+            device_id_type=MESH,
+        )
+
+    own = pltpu.make_async_copy(
+        sent_ref.at[member],
+        out_ref.at[:, pl.ds(pl.multiple_of(member * query_width, query_width), query_width)],
+        send_sem.at[member],
+    )
+    for index in reversed(range(group_size)):
+
+        @pl.when(group > 0)
+        def _():
+            halo(index).wait_recv()
+
+        first = index * row_count
         keys = window_ref[pl.ds(first, reach), :HEAD_DIM]
         values = window_ref[pl.ds(first, reach), HEAD_DIM:]
         visible = near & (key_pos + first + group * span >= span)
@@ -483,44 +519,47 @@
             )
             raw = jnp.where(visible, jnp.exp(scores * score_scale), 0.0)
             probs = (raw * (1.0 / jnp.sum(raw, axis=-1, keepdims=True))).astype(jnp.bfloat16)
-            sent_ref[turn - 1, :, columns] = jnp.dot(
+            sent_ref[index, :, columns] = jnp.dot(
                 probs, values, preferred_element_type=jnp.float32
             ).astype(jnp.bfloat16)
-        mine = out_ref.at[:, pl.ds(pl.multiple_of(member * query_width, query_width), query_width)]
-        if turn < group_size:
-            copy = pltpu.make_async_remote_copy(
-                src_ref=sent_ref.at[turn - 1],
-                dst_ref=mine,
-                send_sem=send_sem.at[turn - 1],
-                recv_sem=recv_sem.at[turn - 1],
-                device_id={"seq": here + index},
-                device_id_type=MESH,
-            )
-        else:
-            copy = pltpu.make_async_copy(sent_ref.at[turn - 1], mine, send_sem.at[turn - 1])
-        copy.start()
-        copies.append(copy)
-    copies[-1].wait()
-    for turn in range(1, group_size):
-        copies[turn - 1].wait_send()
-        origin = lax.rem(member - turn + group_size, group_size)
-        pltpu.make_async_remote_copy(
-            src_ref=sent_ref.at[turn - 1],
-            dst_ref=out_ref.at[
-                :, pl.ds(pl.multiple_of(origin * query_width, query_width), query_width)
-            ],
-            send_sem=send_sem.at[turn - 1],
-            recv_sem=recv_sem.at[turn - 1],
-            device_id={"seq": here + origin},
-            device_id_type=MESH,
-        ).wait_recv()
+
+        @pl.when(member != index)
+        def _():
+            exchange(index, member).start()
+
+        @pl.when(member == index)
+        def _():
+            own.start()
+
+    for index in range(group_size):
+
+        @pl.when(member != index)
+        def _():
+            exchange(index, member).wait_send()
+            exchange(index, index).wait_recv()
+
+        @pl.when(member == index)
+        def _():
+            own.wait()
+
+    held.wait()
+    tile = 384
+
+    @pl.loop(0, partial_ref.shape[1] // tile)
+    def _(index):
+        at = pl.ds(pl.multiple_of(index * tile, tile), tile)
+        partial_ref[:, at] = lax.dot_general(
+            out_ref[...], held_ref[at, :], (((1,), (1,)), ((), ())),
+            preferred_element_type=jnp.float32,
+        ).astype(jnp.bfloat16)
 
     @pl.when(group < groups - 1)
     def _():
-        halo.wait_send()
-
-
-def attend(projected, cosine, sine, group_size):
+        for index in range(group_size):
+            halo(index).wait_send()
+
+
+def attend(projected, cosine, sine, mixes, group_size):
     groups = lax.axis_size("seq") // group_size
     span = projected.shape[0]
     row_count = span // group_size
@@ -529,23 +568,26 @@
     vmem = pl.BlockSpec(memory_space=pltpu.VMEM)
     return pl.pallas_call(
         functools.partial(attend_kernel, groups, group_size, row_count),
-        out_shape=jax.ShapeDtypeStruct((row_count, group_size * query_width), jnp.bfloat16),
-        in_specs=[vmem] * 3,
+        out_shape=jax.ShapeDtypeStruct((row_count, mixes.shape[0]), jnp.bfloat16),
+        in_specs=[vmem] * 3 + [pl.BlockSpec(memory_space=pl.ANY)],
         out_specs=vmem,
         scratch_shapes=[
             pltpu.VMEM((span, query_width), jnp.bfloat16),
             pltpu.VMEM((2 * span, 2 * HEAD_DIM), jnp.bfloat16),
             pltpu.VMEM((group_size, row_count, query_width), jnp.bfloat16),
+            pltpu.VMEM((row_count, group_size * query_width), jnp.bfloat16),
+            pltpu.VMEM(mixes.shape, jnp.bfloat16),
+            dma((group_size,)),
+            dma((group_size,)),
+            dma((group_size,)),
+            dma((group_size,)),
             dma,
-            dma,
-            dma((group_size,)),
-            dma((group_size - 1,)),
         ],
         compiler_params=pltpu.CompilerParams(
             collective_id=1, has_side_effects=True, vmem_limit_bytes=40 * 1024 * 1024
         ),
         name="attend",
-    )(projected, cosine, sine)
+    )(projected, cosine, sine, mixes)
 
 
 def finish_kernel(
@@ -642,15 +684,13 @@
 
     def attend_layer(weights, tokens, residual_half):
         projected = jnp.dot(tokens, weights, preferred_element_type=jnp.float32)
-        attended = attend(projected, cosine, sine, group_size)
-        partial_value = lax.dot_general(
-            attended, mixes, (((1,), (1,)), ((), ())), preferred_element_type=jnp.float32
-        ).astype(jnp.bfloat16)
+        partial_value = attend(projected, cosine, sine, mixes, group_size)
         return finish(partial_value, residual_half, gain_second)
 
     own_half = lax.dynamic_slice_in_dim(hidden_in, core_index * half_width, half_width, 1)
     weights, tokens, mixes = gather(
-        normed_rows(hidden_in),
+        hidden_in,
+        gain_first,
         query_weight[0],
         key_weight[0],
         value_weight[0],

time: 216 us -> 206 us (0.954)
  matrix products: 21.8 us -> 7.2 us
  other arithmetic: 9.6 us -> 3.02 us
  local copies, waits for them, and re-layouts: 2.53 us -> 8.46 us
  Pallas kernels: 182 us -> 187 us
    dot_general x1 -> x0, matrix products: 11.5 us -> none  [attend_layer(): lax.dot_general(attended, mixes, (((1,), (1,)), ((), ())), preferred_elem...]
    unnamed x3 -> x15, local copies, waits for them, and re-layouts: 1.09 us -> 7.02 us
    pallas_call x1, Pallas kernels: 21.4 us -> 25.2 us  [attend(): pl.pallas_call(functools.partial(attend_kernel, groups, group_size, row_c...]
    convert_element_type x1, other arithmetic: 4.13 us -> 0.75 us  [body(): gain_first = input_gain[0].astype(jnp.float32)]
    dot_general x1, matrix products: 10.2 us -> 7.2 us  [attend_layer(): projected = jnp.dot(tokens, weights, preferred_element_type=jnp.float32)]
    reduce_sum x1 -> x0, other arithmetic: 2.4 us -> none  [normed_rows(): jnp.mean(rows_float * rows_float, axis=1, keepdims=True) + NORM_EPS]
where the time goes in v3:
time: 206 us
  Pallas kernels  187 us (91%)
  local copies, waits for them, and re-layouts  8.46 us (4%)
  matrix products  7.2 us (3%)
  other arithmetic  3.02 us (1%)
    pallas_call x1, Pallas kernels, gather(): pl.pallas_call(functools.partial(gather_kernel, groups, group_size), out_...  152 us
    pallas_call x1, Pallas kernels, attend(): pl.pallas_call(functools.partial(attend_kernel, groups, group_size, row_c...  25.2 us
    pallas_call x1, Pallas kernels, finish(): pl.pallas_call(finish_kernel, out_shape=jax.ShapeDtypeStruct((row_count,...  9.63 us
    dot_general x1, matrix products, attend_layer(): projected = jnp.dot(tokens, weights, preferred_element_type=jnp.float32)  7.2 us
    unnamed x15, local copies, waits for them, and re-layouts  7.02 us

profile of v3, /device:TPU:9, one launch (start us, length us, event | category | flops | bytes accessed | tf_op | source)
XLA Modules:
  0.0 205.8 jit_solution(16175553160163698073)
XLA Ops:
  0.0 0.8 convert_element_type.15.gain_ref
  0.8 0.0 copy-start
  0.8 1.8 copy-done
  2.5 0.0 copy-start.2
  2.5 1.1 copy-done.2
  3.6 0.0 copy-start.3
  3.6 1.1 copy-done.3
  4.7 0.0 copy-start.4
  4.7 1.0 copy-done.4
  5.7 0.0 copy-start.5
  5.7 1.0 copy-done.5
  6.7 152.3 %gather.1 = (bf16[16,336,512]{2,1,0:T(8,128)(2,1)S(1)}, bf16[4,2,128,5376]{3,2,1,0:T(8,128)(2,1)S(1)}, bf16[16,336,1024]{2,1,0:T(8,128)(2,1)}) custom-call(bf16[2,128,5376]{2,1,0:T(8,128)(2,1)S(1)} %bitcast.13, f32[1,5376]{1,0:T(1,128)S(1)} %convert_element_type.15.gain_ref, bf16[336,1024]{1,0:T(8,128)(2,1)S(1)} %bitcast.15, bf16[336,512]{1,0:T(8,128)(2,1)S(1)} %bitcast.17, ...), custom_call_target="tpu_custom_call" | custom-call | tf_op jit(solution)/shard_map/gather/pallas_call | solution.py:373
  159.0 7.2 %fusion.1.projected_ref = f32[1024,512]{1,0:T(8,128)} fusion(bf16[1024,5376]{1,0:T(8,128)(2,1)S(1)} %bitcast.19, bf16[5376,512]{1,0:T(8,128)(2,1)S(1)} %bitcast.20), kind=kOutput, calls=%fused_computation.8 | convolution fusion | flops 5637144576 | bytes 18612224 | tf_op jit(solution)/shard_map/dot_general | solution.py:686
  166.2 0.0 copy-start.1
  166.2 1.9 fusion
  168.1 0.3 pad_maximum_fusion
  168.4 0.0 copy-done.1
  168.4 0.0 copy-start.6
  168.5 25.2 %attend.1.partial_ref = bf16[256,5376]{1,0:T(8,128)(2,1)S(1)} custom-call(f32[1024,512]{1,0:T(8,128)S(1)} %copy-done.1, f32[1024,128]{1,0:T(8,128)S(1)} %get-tuple-element.14.cosine_ref, f32[1024,128]{1,0:T(8,128)S(1)} %get-tuple-element.15.sine_ref, bf16[5376,1024]{1,0:T(8,128)(2,1)} %bitcast.21), custom_call_target="tpu_custom_call" | custom-call | tf_op jit(solution)/shard_map/attend/pallas_call | solution.py:569
  193.6 1.4 constant_dynamic-slice_fusion.residual_ref
  195.1 0.0 copy-done.6
  195.1 9.6 %finish.1 = bf16[256,2688]{1,0:T(8,128)(2,1)S(1)} custom-call(bf16[256,5376]{1,0:T(8,128)(2,1)S(1)} %attend.1.partial_ref, bf16[256,2688]{1,0:T(8,128)(2,1)S(1)} %constant_dynamic-slice_fusion.residual_ref, f32[1,2688]{1,0:T(1,128)S(1)} %convert_element_type.17.gain_ref), custom_call_target="tpu_custom_call" | custom-call | tf_op jit(solution)/shard_map/finish/pallas_call | solution.py:640
  204.7 1.1 copy.9
  (3 shorter events, 0.0 us)
Async XLA Ops:
  0.8 1.8 copy-start
  2.5 1.1 copy-start.2
  3.6 1.1 copy-start.3
  4.7 1.0 copy-start.4
  5.7 1.0 copy-start.5
  166.2 2.3 %copy-start.1 = (f32[1024,512]{1,0:T(8,128)S(1)}, f32[1024,512]{1,0:T(8,128)}, u32[]{:S(2)}) copy-start(f32[1024,512]{1,0:T(8,128)} %fusion.1.projected_ref) | copy-start | bytes 6291460
  168.4 26.6 %copy-start.6 = (bf16[1,2688]{1,0:T(2,128)(2,1)S(1)}, bf16[1,2688]{1,0:T(2,128)(2,1)}, u32[]{:S(2)}) copy-start(bf16[1,2688]{1,0:T(2,128)(2,1)} %param.13) | copy-start | bytes 16132

commit v4 on v3

--- a/solution.py
+++ b/solution.py
@@ -40,11 +40,11 @@
 
 
 def gather_kernel(
-    groups, group_size, hidden_ref, gain_ref, query_ref, key_ref, value_ref, mix_ref,
+    groups, group_size, source_ref, gain_ref, query_ref, key_ref, value_ref, mix_ref,
     weights_ref, tokens_ref, mixes_ref,
     own_sem, plane_send, plane_recv, token_send, token_recv, twin_send, twin_recv,
     up_send, up_recv, down_send, down_recv,
-    side_send, side_recv, pass_send, pass_recv, rows_ref,
+    side_send, side_recv, pass_send, pass_recv, rows_ref, hidden_ref,
 ):
     group, member, core = place(group_size)
     here = group * group_size
@@ -70,6 +70,8 @@
         group_size + jnp.where(group > 0, 1, 0) + jnp.where(group < groups - 1, 1, 0),
     )
 
+    fetch = pltpu.make_async_copy(source_ref, hidden_ref, own_sem.at[5])
+    fetch.start()
     sources = (query_ref, key_ref, value_ref)
     widths = [ref.shape[1] // group_size for ref in sources]
     starts = [0, widths[0], widths[0] + widths[1]]
@@ -259,6 +261,7 @@
         return group - step >= 0 if upward else group + step <= groups - 1
 
     mix_step(0)
+    fetch.wait()
     chunk = 16
     for half in range(2):
 
@@ -301,6 +304,7 @@
                 def _():
                     relay(step, d, upward).start()
 
+        mix_step(step)
         if step == 1:
             token_direct(1, flipped(1)).wait_recv()
             token_half(flipped(1), 0, 2).start()
@@ -308,8 +312,7 @@
             token_direct(2, flipped(2)).wait_recv()
             token_half(flipped(2), 1, 1).start()
             twin(1, core).start()
-        mix_step(step)
-        if step == 1:
+        if step == min(2, groups - 1):
             token_half(flipped(3), 0, 2).wait_recv()
             twin(2, core).start()
             token_half(flipped(3), 1, 1).wait_recv()
@@ -377,10 +380,10 @@
             jax.ShapeDtypeStruct((group_size,) + halves.shape, jnp.bfloat16),
             jax.ShapeDtypeStruct((shards,) + mix_weight.shape, jnp.bfloat16),
         ),
-        in_specs=[pl.BlockSpec(memory_space=pltpu.VMEM)] * 2 + [anywhere] * 4,
+        in_specs=[anywhere, pl.BlockSpec(memory_space=pltpu.VMEM)] + [anywhere] * 4,
         out_specs=(anywhere, anywhere, anywhere),
         scratch_shapes=[
-            dma((5,)),
+            dma((6,)),
             dma((group_size - 1, 3)),
             dma((group_size - 1, 3)),
             dma((4,)),
@@ -395,6 +398,7 @@
             dma((2, groups)),
             dma((2, groups)),
             dma((2, groups)),
+            pltpu.VMEM(halves.shape, jnp.bfloat16),
             pltpu.VMEM(halves.shape, jnp.bfloat16),
         ],
         compiler_params=pltpu.CompilerParams(

time: 206 us -> 206 us (level)
    pallas_call x1, Pallas kernels: 25.2 us -> 29.1 us  [attend(): pl.pallas_call(functools.partial(attend_kernel, groups, group_size, row_c...]
    pallas_call x1, Pallas kernels: 9.63 us -> 6.03 us  [finish(): pl.pallas_call(finish_kernel, out_shape=jax.ShapeDtypeStruct((row_count,...]
where the time goes in v4:
time: 206 us
  Pallas kernels  187 us (91%)
  local copies, waits for them, and re-layouts  8.46 us (4%)
  matrix products  7.2 us (3%)
  other arithmetic  3.02 us (1%)
    pallas_call x1, Pallas kernels, gather(): pl.pallas_call(functools.partial(gather_kernel, groups, group_size), out_...  152 us
    pallas_call x1, Pallas kernels, attend(): pl.pallas_call(functools.partial(attend_kernel, groups, group_size, row_c...  29.1 us
    dot_general x1, matrix products, attend_layer(): projected = jnp.dot(tokens, weights, preferred_element_type=jnp.float32)  7.2 us
    unnamed x15, local copies, waits for them, and re-layouts  7.02 us
    pallas_call x1, Pallas kernels, finish(): pl.pallas_call(finish_kernel, out_shape=jax.ShapeDtypeStruct((row_count,...  6.03 us

profile of v4, /device:TPU:9, one launch (start us, length us, event | category | flops | bytes accessed | tf_op | source)
XLA Modules:
  0.0 205.9 jit_solution(17304079706320280323)
XLA Ops:
  0.0 0.8 convert_element_type.15.gain_ref
  0.8 0.0 copy-start
  0.8 1.8 copy-done
  2.5 0.0 copy-start.2
  2.5 1.1 copy-done.2
  3.6 0.0 copy-start.3
  3.6 1.1 copy-done.3
  4.7 0.0 copy-start.4
  4.7 1.0 copy-done.4
  5.7 0.0 copy-start.5
  5.7 1.0 copy-done.5
  6.7 152.0 %gather.1 = (bf16[16,336,512]{2,1,0:T(8,128)(2,1)S(1)}, bf16[4,2,128,5376]{3,2,1,0:T(8,128)(2,1)S(1)}, bf16[16,336,1024]{2,1,0:T(8,128)(2,1)}) custom-call(bf16[2,128,5376]{2,1,0:T(8,128)(2,1)S(1)} %bitcast.13, f32[1,5376]{1,0:T(1,128)S(1)} %convert_element_type.15.gain_ref, bf16[336,1024]{1,0:T(8,128)(2,1)S(1)} %bitcast.15, bf16[336,512]{1,0:T(8,128)(2,1)S(1)} %bitcast.17, ...), custom_call_target="tpu_custom_call" | custom-call | tf_op jit(solution)/shard_map/gather/pallas_call | solution.py:376
  158.7 7.2 %fusion.1.projected_ref = f32[1024,512]{1,0:T(8,128)} fusion(bf16[1024,5376]{1,0:T(8,128)(2,1)S(1)} %bitcast.19, bf16[5376,512]{1,0:T(8,128)(2,1)S(1)} %bitcast.20), kind=kOutput, calls=%fused_computation.8 | convolution fusion | flops 5637144576 | bytes 18612224 | tf_op jit(solution)/shard_map/dot_general | solution.py:690
  165.9 0.0 copy-start.1
  165.9 1.9 fusion
  167.8 0.3 pad_maximum_fusion
  168.1 0.0 copy-done.1
  168.1 0.0 copy-start.6
  168.2 29.1 %attend.1.partial_ref = bf16[256,5376]{1,0:T(8,128)(2,1)S(1)} custom-call(f32[1024,512]{1,0:T(8,128)S(1)} %copy-done.1, f32[1024,128]{1,0:T(8,128)S(1)} %get-tuple-element.14.cosine_ref, f32[1024,128]{1,0:T(8,128)S(1)} %get-tuple-element.15.sine_ref, bf16[5376,1024]{1,0:T(8,128)(2,1)} %bitcast.21), custom_call_target="tpu_custom_call" | custom-call | tf_op jit(solution)/shard_map/attend/pallas_call | solution.py:573
  197.3 1.4 constant_dynamic-slice_fusion.residual_ref
  198.7 0.0 copy-done.6
  198.8 6.0 %finish.1 = bf16[256,2688]{1,0:T(8,128)(2,1)S(1)} custom-call(bf16[256,5376]{1,0:T(8,128)(2,1)S(1)} %attend.1.partial_ref, bf16[256,2688]{1,0:T(8,128)(2,1)S(1)} %constant_dynamic-slice_fusion.residual_ref, f32[1,2688]{1,0:T(1,128)S(1)} %convert_element_type.17.gain_ref), custom_call_target="tpu_custom_call" | custom-call | tf_op jit(solution)/shard_map/finish/pallas_call | solution.py:644
  204.8 1.1 copy.9
  (3 shorter events, 0.0 us)
Async XLA Ops:
  0.8 1.8 copy-start
  2.5 1.1 copy-start.2
  3.6 1.1 copy-start.3
  4.7 1.0 copy-start.4
  5.7 1.0 copy-start.5
  165.9 2.3 %copy-start.1 = (f32[1024,512]{1,0:T(8,128)S(1)}, f32[1024,512]{1,0:T(8,128)}, u32[]{:S(2)}) copy-start(f32[1024,512]{1,0:T(8,128)} %fusion.1.projected_ref) | copy-start | bytes 6291460
  168.1 30.6 %copy-start.6 = (bf16[1,2688]{1,0:T(2,128)(2,1)S(1)}, bf16[1,2688]{1,0:T(2,128)(2,1)}, u32[]{:S(2)}) copy-start(bf16[1,2688]{1,0:T(2,128)(2,1)} %param.13) | copy-start | bytes 16132
